TPU v7x, 32 devices: a whole 2x2x4 slice. The times are simulated.
32 devices in a mesh: req: 2 (over core), seq: 16 (over z, y, x).
Axes of the slice: x: 2, y: 2, z: 4, core: 2. Of those that a mesh axis runs over, the one named last changes fastest.
Arguments:
- tokens: bfloat16 [4, 32, 1536], P(None, ('req', 'seq')), may hold values from -6 to 6
- lengths: int32 [32], P('req'), may hold values from 1 to 16384, as said below
- k_cache: bfloat16 [32, 4096, 256], P('req', 'seq'), may hold values from -500 to 500
- v_cache: bfloat16 [32, 4096, 256], P('req', 'seq'), may hold values from -12 to 12
- attn_gain: bfloat16 [1536], replicated, may hold values from 0.5 to 1.5
- w_qkv: bfloat16 [1536, 2048], replicated, may hold values from -0.15625 to 0.15625
- sink: float32 [12], replicated, may hold values from -1 to 3
- w_out: bfloat16 [1536, 1536], replicated, may hold values from -0.15625 to 0.15625
- moe_gain: bfloat16 [1536], replicated, may hold values from 0.5 to 1.5
- router: bfloat16 [1536, 32], replicated, may hold values from -0.15625 to 0.15625
- w_gate: bfloat16 [1536, 24576], P(None, ('req', 'seq')), may hold values from -0.15625 to 0.15625
- w_up: bfloat16 [1536, 24576], P(None, ('req', 'seq')), may hold values from -0.15625 to 0.15625
- w_down: bfloat16 [24576, 1536], P(('req', 'seq')), may hold values from -0.21875 to 0.21875
- routes: int32 [32, 4, 4], replicated, may hold values from 0 to 31, all different within a row; in each aligned block of 4 rows (0 to 3, 4 to 7, ..., all dimensions but the last counted through in order) at most 2 rows name the same one
Outputs:
- outputs: bfloat16 [4, 32, 1536], P(None, ('req', 'seq'))
Inputs may be any that keep to these rules, and one draw needn't show every extreme that they name: Each request has lengths positions before the first step; some request has all 16384 in every draw. `routes`: among the 4 tokens of one device's requests (requests 1 d .. 1 d + 1 - 1, all steps), no expert is named by more than 2 tokens, and in every draw some expert is named by exactly 2.
All inputs are finite; a program needn't handle non-finite values.
Results may differ from a plain program's by a relative error of at most 0.02.
Values may be sent and summed in bfloat16 or wider, within the bound.
A program may use at most 512 MiB of HBM per device.

v0:
```python
import jax
import jax.numpy as jnp
from jax import lax
from jax.sharding import PartitionSpec as P

D = 1536
QH = 12
KVH = 2
HD = 128
E = 32
EFF = 768
TOP = 4
STEPS = 4
MOST = 2


def combined_all(value, axis, join):
    gathered = jax.tree.map(
        lambda a, kind: lax.all_gather(a.astype(kind), axis),
        value,
        (jnp.bfloat16, jnp.bfloat16, jnp.bfloat16),
    )

    def take(source):
        return jax.tree.map(
            lambda a, own: lax.dynamic_index_in_dim(a, source, 0, False).astype(own.dtype),
            gathered,
            value,
        )

    return lax.fori_loop(
        1, lax.axis_size(axis), lambda source, state: join(state, take(source)), take(0)
    )


def normalize(x, gain):
    xf = x.astype(jnp.float32)
    inv = lax.rsqrt(jnp.mean(xf * xf, axis=-1, keepdims=True) + 1e-05)
    return (xf * inv * gain.astype(jnp.float32)).astype(jnp.bfloat16)


def rotate(x, place):
    half = x.shape[-1] // 2
    index = jnp.arange(half, dtype=jnp.float32)
    inverse = jnp.exp(-jnp.log(1000000.0) * 2.0 * index / x.shape[-1])
    angle = place.astype(jnp.float32)[..., None, None] * inverse
    first = x[..., :half]
    second = x[..., half:]
    cosine = jnp.cos(angle)
    sine = jnp.sin(angle)
    return jnp.concatenate(
        [first * cosine - second * sine, second * cosine + first * sine], axis=-1
    )


def route_weights(logits, picks):
    onehot = (picks[:, :, None] == jnp.arange(E, dtype=jnp.int32)[None, None, :]).astype(
        jnp.float32
    )
    chosen = jnp.sum(onehot * logits[:, None, :], axis=-1)
    share = jax.nn.softmax(chosen, axis=-1)
    return jnp.sum(share[:, :, None] * onehot, axis=1)


def combine_parts(first, second):
    peak = jnp.maximum(first[0], second[0])
    left_scale = jnp.exp(first[0] - peak)
    right_scale = jnp.exp(second[0] - peak)
    return (
        peak,
        first[1] * left_scale + second[1] * right_scale,
        first[2] * left_scale[..., None] + second[2] * right_scale[..., None],
    )


def on_device(
    tokens,
    lengths,
    k_cache,
    v_cache,
    attn_gain,
    w_qkv,
    sink,
    w_out,
    moe_gain,
    router,
    w_gate,
    w_up,
    w_down,
    routes,
):
    seq_count = lax.axis_size("seq")
    seq_place = lax.axis_index("seq")
    device = lax.axis_index("req") * seq_count + seq_place
    devices = lax.axis_size(("req", "seq"))
    rows = tokens.shape[1]
    group_rows = lengths.shape[0]
    local_pos = k_cache.shape[1]
    window = local_pos * seq_count
    heads_per = QH // KVH
    scale = HD ** (-0.5)
    columns = w_gate.shape[1]
    expert_mine = device * columns // EFF
    own_len = lax.dynamic_slice_in_dim(lengths, seq_place * rows, rows)
    step_ids = jnp.arange(STEPS, dtype=jnp.int32)
    a = normalize(tokens, attn_gain)
    proj = jnp.einsum("srm,mn->srn", a, w_qkv, preferred_element_type=jnp.float32)
    place = own_len[None, :] + step_ids[:, None]
    query = rotate(proj[..., : QH * HD].reshape(STEPS, rows, QH, HD), place).astype(jnp.bfloat16)
    fresh_key = rotate(
        proj[..., QH * HD : (QH + KVH) * HD].reshape(STEPS, rows, KVH, HD), place
    ).astype(jnp.bfloat16)
    fresh_val = proj[..., (QH + KVH) * HD :].reshape(STEPS, rows, KVH, HD).astype(jnp.bfloat16)
    every_query = lax.all_gather(query.reshape(STEPS, rows, QH * HD), "seq", axis=1, tiled=True)
    grouped_all = every_query.reshape(STEPS, group_rows, KVH, heads_per, HD)
    cache_keys = k_cache.reshape(group_rows, local_pos, KVH, HD)
    cache_vals = v_cache.reshape(group_rows, local_pos, KVH, HD)
    scores = (
        jnp.einsum("tnkgd,nckd->tnkgc", grouped_all, cache_keys, preferred_element_type=jnp.float32)
        * scale
    )
    key_slot = seq_place * local_pos + jnp.arange(local_pos, dtype=jnp.int32)
    back = jnp.mod(lengths[None, :, None] - 1 - key_slot[None, None, :], window)
    reach = jnp.minimum(lengths[None, :, None], window - 1 - step_ids[:, None, None])
    valid = (back < reach)[:, :, None, None, :]
    peak_local = jnp.max(jnp.where(valid, scores, -1e30), axis=-1)
    weights = jnp.where(valid, jnp.exp(scores - peak_local[..., None]), 0.0)
    total_local = jnp.sum(weights, axis=-1)
    mixed_local = jnp.einsum(
        "tnkgc,nckd->tnkgd",
        weights.astype(jnp.bfloat16),
        cache_vals,
        preferred_element_type=jnp.float32,
    )
    peak_all, total_all, mixed_all = combined_all(
        (peak_local, total_local, mixed_local), "seq", combine_parts
    )
    peak = lax.dynamic_slice_in_dim(peak_all, seq_place * rows, rows, 1)
    total = lax.dynamic_slice_in_dim(total_all, seq_place * rows, rows, 1)
    mixed = lax.dynamic_slice_in_dim(mixed_all, seq_place * rows, rows, 1)
    grouped = query.reshape(STEPS, rows, KVH, heads_per, HD)
    tail_scores = (
        jnp.einsum("trkgd,srkd->trkgs", grouped, fresh_key, preferred_element_type=jnp.float32)
        * scale
    )
    tail_valid = (step_ids[None, :] <= step_ids[:, None])[:, None, None, None, :]
    sink_grid = sink.reshape(KVH, heads_per)[None, None]
    final = jnp.maximum(
        jnp.maximum(peak, jnp.max(jnp.where(tail_valid, tail_scores, -1e30), axis=-1)), sink_grid
    )
    shift = jnp.exp(peak - final)
    tail_w = jnp.where(tail_valid, jnp.exp(tail_scores - final[..., None]), 0.0)
    denom = total * shift + jnp.sum(tail_w, axis=-1) + jnp.exp(sink_grid - final)
    mixed = mixed * shift[..., None] + jnp.einsum(
        "trkgs,srkd->trkgd",
        tail_w.astype(jnp.bfloat16),
        fresh_val,
        preferred_element_type=jnp.float32,
    )
    attn = (mixed / denom[..., None]).reshape(STEPS, rows, QH * HD).astype(jnp.bfloat16)
    h = (
        tokens.astype(jnp.float32)
        + jnp.einsum("srn,nm->srm", attn, w_out, preferred_element_type=jnp.float32)
    ).astype(jnp.bfloat16)
    u = normalize(h, moe_gain)
    own_tokens = rows * STEPS
    u_tok = u.transpose(1, 0, 2).reshape(own_tokens, D)
    every_row = lax.all_gather(u_tok, ("req", "seq"), axis=0, tiled=True)
    all_picks = routes.reshape(-1, TOP)
    every_logit = jnp.dot(every_row, router, preferred_element_type=jnp.float32)
    dense_all = route_weights(every_logit, all_picks)
    weight_mine = jnp.sum(
        dense_all * (jnp.arange(E, dtype=jnp.int32) == expert_mine)[None, :].astype(jnp.float32),
        axis=-1,
    )
    mine = jnp.any(all_picks == expert_mine, axis=-1)
    slot = jnp.cumsum(mine.astype(jnp.int32)) - 1
    limit = MOST * devices
    select = (
        (slot[None, :] == jnp.arange(limit, dtype=jnp.int32)[:, None]) & mine[None, :]
    ).astype(jnp.float32)
    picked = jnp.dot(
        select.astype(jnp.bfloat16), every_row, preferred_element_type=jnp.float32
    ).astype(jnp.bfloat16)
    slot_weight = jnp.dot(select, weight_mine, precision=lax.Precision.HIGHEST)
    hidden = (
        jax.nn.relu(jnp.dot(picked, w_gate, preferred_element_type=jnp.float32))
        * jnp.dot(picked, w_up, preferred_element_type=jnp.float32)
    ).astype(jnp.bfloat16)
    produced = jnp.dot(hidden, w_down, preferred_element_type=jnp.float32) * slot_weight[:, None]
    moe = lax.psum_scatter(
        jnp.einsum("lc,lm->cm", select, produced, precision=lax.Precision.HIGHEST),
        ("req", "seq"),
        scatter_dimension=0,
        tiled=True,
    )
    moe_steps = moe.reshape(rows, STEPS, D).transpose(1, 0, 2)
    return (h.astype(jnp.float32) + moe_steps).astype(jnp.bfloat16)


def solution(mesh):
    in_specs = (
        P(None, ("req", "seq"), None),
        P("req"),
        P("req", "seq", None),
        P("req", "seq", None),
        P(),
        P(),
        P(),
        P(),
        P(),
        P(),
        P(None, ("req", "seq")),
        P(None, ("req", "seq")),
        P(("req", "seq"), None),
        P(),
    )
    out_specs = P(None, ("req", "seq"), None)
    return jax.shard_map(
        on_device, mesh=mesh, in_specs=in_specs, out_specs=out_specs, check_vma=False
    )
```

profile of v0, /device:TPU:0, one launch (start us, length us, event | category | flops | bytes accessed | tf_op | source)
XLA Modules:
  0.0 411.4 jit_solution(13245139191897642980)
XLA Ops:
  8.3 3.8 convolution_bitcast_fusion.1
  14.0 4.0 reshape.433
  18.3 43.4 %all_gather.20 = bf16[4,16,1536]{2,0,1:T(4,128)(2,1)S(1)} all-gather(bf16[4,1,1536]{2,0,1:T(4,128)(2,1)S(1)} %convert_element_type.206), channel_id=1, replica_groups=mesh['req'=2,'seq'=16] {'seq'}, dimensions={1}, use_global_device_ids=true | all-gather | bytes 208896 | tf_op jit(solution)/shard_map/all_gather | solution.py:114
  62.5 4.0 reshape.434
  66.7 2.6 select_reduce_fusion
  85.0 37.8 %all-gather = bf16[64,16,2,6]{1,2,3,0:T(2,128)(2,1)S(1)} all-gather(bf16[4,16,2,6]{1,2,3,0:T(2,128)(2,1)} %copy.163), channel_id=2, replica_groups=mesh['req'=2,'seq'=16] {'seq'}, dimensions={0}, use_global_device_ids=true | all-gather | bytes 26112 | tf_op jit(solution)/shard_map/all_gather | solution.py:19
  122.8 39.5 %all-gather.1 = bf16[64,16,2,6]{1,2,3,0:T(2,128)(2,1)S(1)} all-gather(bf16[4,16,2,6]{1,2,3,0:T(2,128)(2,1)S(1)} %copy.165), channel_id=3, replica_groups=mesh['req'=2,'seq'=16] {'seq'}, dimensions={0}, use_global_device_ids=true | all-gather | bytes 26112 | tf_op jit(solution)/shard_map/all_gather | solution.py:19
  164.4 1.6 select_reduce_fusion.3
  167.3 27.1 %while.19 = (s32[]{:T(128)}, f32[4,16,2,6]{1,2,3,0:T(2,128)S(1)}, f32[4,16,2,6]{1,2,3,0:T(2,128)S(1)}, f32[4,16,2,6,128]{4,3,2,1,0:T(8,128)S(1)}, bf16[16,4,16,2...) while((s32[]{:T(128)}, f32[4,16,2,6]{1,2,3,0:T(2,128)S(1)}, ...), condition=%wide.region_4.5_spmd, body=%wide.region_3.4_spmd.sunk | while | flops 399365 | bytes 1088663 | solution.py:31
  167.6 1.4 fusion.101
  171.2 1.4 fusion.101
  173.0 1.4 fusion.101
  174.8 1.4 fusion.101
  176.6 1.4 fusion.101
  178.4 1.4 fusion.101
  185.7 1.4 fusion.101
  187.5 1.4 fusion.101
  189.3 1.4 fusion.101
  191.1 1.4 fusion.101
  197.8 3.2 multiply_reduce_fusion
  201.1 67.8 %all-gather.3 = bf16[128,1,1536]{2,1,0:T(2,128)(2,1)S(1)} all-gather(bf16[4,1,1536]{2,1,0:T(2,128)(2,1)S(1)} %copy.188), channel_id=5, replica_groups=mesh['req'=2,'seq'=16] {'req','seq'}, dimensions={0}, use_global_device_ids=true | all-gather | bytes 405504 | tf_op jit(solution)/shard_map/all_gather | solution.py:168
  269.8 2.2 convolution_maximum_fusion
  272.0 2.8 convolution_multiply_fusion
  276.2 126.9 %all-reduce.3.cloned.1.call-done = f32[128,1536]{1,0:T(8,128)} async-done(((f32[128,1536]{1,0:T(8,128)}), f32[128,1536]{1,0:T(8,128)}) %all-reduce.3.cloned.1.call-update) | async-done | bytes 786448
  (155 shorter events, 43.1 us)
Async XLA Ops:
  6.5 265.5 %copy-start = (bf16[768,1536]{1,0:T(8,128)(2,1)S(1)}, bf16[768,1536]{1,0:T(8,128)(2,1)}, u32[]{:S(2)}) copy-start(bf16[768,1536]{1,0:T(8,128)(2,1)} %param.28) | copy-start | bytes 7077892
  6.5 159.6 %all-gather.6.cloned.1.call-start = ((), (), s32[]{:S(2)}) async-start(), calls=%async_computation | async-start | bytes 4456448 | tf_op jit(solution)/shard_map/all_gather | solution.py:19
  8.2 4.4 %copy-start.9 = (s32[16]{0:T(128)S(1)}, s32[16]{0:T(128)}, u32[]{:S(2)}) copy-start(s32[16]{0:T(128)} %param.17) | copy-start | bytes 196
  12.0 0.6 copy-start.2
  18.1 44.4 %copy-start.5 = (f32[4,64]{1,0:T(4,128)}, f32[4,64]{1,0:T(4,128)S(1)}, u32[]{:S(2)}) copy-start(f32[4,64]{1,0:T(4,128)S(1)} %get-tuple-element.252) | copy-start | bytes 3076
  18.1 44.4 %copy-start.6 = (f32[4,64]{1,0:T(4,128)}, f32[4,64]{1,0:T(4,128)S(1)}, u32[]{:S(2)}) copy-start(f32[4,64]{1,0:T(4,128)S(1)} %get-tuple-element.253) | copy-start | bytes 3076
  66.5 2.8 copy-start.1
  69.2 3.3 copy-start.4
  70.6 332.6 %all-reduce.3.cloned.1.call-start = ((), (), s32[]{:S(2)}) async-start(), calls=%async_computation.1 | async-start | bytes 1572864
  162.3 4.9 %copy-start.11 = (pred[4,4]{1,0:T(4,128)(4,1)}, pred[4,4]{1,0:T(4,128)(4,1)S(1)}, u32[]{:S(2)}) copy-start(pred[4,4]{1,0:T(4,128)(4,1)S(1)} %iota_compare_fusion.2) | copy-start | bytes 52
  167.2 27.2 %copy-start.8 = (f32[2,6]{1,0:T(2,128)S(1)}, f32[2,6]{1,0:T(2,128)}, u32[]{:S(2)}) copy-start(f32[2,6]{1,0:T(2,128)} %max.34) | copy-start | bytes 148
  167.2 30.5 %copy-start.3 = (bf16[4,1,1536]{2,0,1:T(4,128)(2,1)S(1)}, bf16[4,1,1536]{2,0,1:T(4,128)(2,1)}, u32[]{:S(2)}) copy-start(bf16[4,1,1536]{2,0,1:T(4,128)(2,1)} %param.16) | copy-start | bytes 36868
  197.8 71.2 %copy-start.12 = (bf16[1536,32]{0,1:T(8,128)(2,1)S(1)}, bf16[1536,32]{0,1:T(8,128)(2,1)}, u32[]{:S(2)}) copy-start(bf16[1536,32]{0,1:T(8,128)(2,1)} %param.25) | copy-start | bytes 294916
  197.8 71.5 %copy-start.7 = (pred[128]{0:T(512)(128)(4,1)S(1)}, pred[128]{0:T(512)(128)(4,1)}, u32[]{:S(2)}) copy-start(pred[128]{0:T(512)(128)(4,1)} %and.31) | copy-start | bytes 388
  197.8 71.8 %copy-start.10 = (f32[32]{0:T(128)S(1)}, f32[32]{0:T(128)}, u32[]{:S(2)}) copy-start(f32[32]{0:T(128)} %compare_convert_fusion) | copy-start | bytes 388
Sparse Core Ops, SparseCore 0:
  70.7 79.7 all-gather.5
  276.3 126.7 all-reduce.2
where the time goes:
time: 413 us; the launch traced here: 411 us
  blocking collectives  189 us (46%)
  waiting for transfers between devices  127 us (31%)
  other arithmetic  34.5 us (8%)
  local copies, waits for them, and re-layouts  26.8 us (6%)
  matrix products  20.3 us (5%)
  between operations  13.8 us (3%)
    unnamed x3, waiting for transfers between devices  127 us
    all_gather x2, blocking collectives, combined_all(): lax.all_gather(a.astype(kind), axis)  77.3 us
    all_gather x1, blocking collectives, on_device(): every_row = lax.all_gather(u_tok, ('req', 'seq'), axis=0, tiled=True)  67.8 us
    all_gather x1, blocking collectives, on_device(): lax.all_gather(query.reshape(STEPS, rows, QH * HD), 'seq', axis=1, tiled=...  43.4 us
    add x15, other arithmetic, combine_parts(): first[2] * left_scale[..., None] + second[2] * right_scale[..., None]  21.7 us
  transfers between devices with their start and end apart: 2, of which 1 were waited for; matrix products, arithmetic and copies ran while one was open for 4% of the time, Pallas kernels for 0%

commit v1 on v0

v1 whole, which is shorter than its diff:
```python
import functools

import jax
import jax.numpy as jnp
from jax import lax
from jax.experimental import pallas as pl
from jax.experimental.pallas import tpu as pltpu
from jax.sharding import PartitionSpec as P

D = 1536
QH = 12
KVH = 2
HD = 128
E = 32
EFF = 768
TOP = 4
STEPS = 4
MOST = 2

ROWS = QH * STEPS
HALF = ROWS // KVH
MSG = ROWS + 16
UG = 4
UL = D // UG
OG = 6
OL = D // OG
BLK = 32
MESH = pl.DeviceIdType.MESH
F32 = jnp.float32
BF16 = jnp.bfloat16


def iota(shape, axis):
    return lax.broadcasted_iota(jnp.int32, shape, axis)


def normed(xf, gain):
    inv = lax.rsqrt(jnp.mean(xf * xf, axis=-1, keepdims=True) + 1e-05)
    return xf * inv * gain


def split3(v):
    hi = v.astype(BF16).astype(F32)
    mid = (v - hi).astype(BF16).astype(F32)
    return hi, mid, v - hi - mid


def kernel(
    nr, ns, blk, lens, x_ref, again_ref, mgain_ref, rope_ref, sink_ref, rall_ref, rown_ref, router_ref,
    kc_hbm, vc_hbm, wqkv_hbm, wout_hbm, wg_hbm, wu_hbm, wd_hbm,
    out_ref,
    wqkv, wout, wg, wu, wd, kc, vc,
    qf, kf, vf, q_all, part, part_in, uf, rows_all, prod_out, prod_in, coef,
    wsem, q_s, q_r, p_s, p_r, u_s, u_r, f_s, o_s, o_r,
):
    devs = nr * ns
    req = lax.axis_index("req")
    seq = lax.axis_index("seq")
    me = req * ns + seq
    lpos = kc.shape[1]
    window = lpos * ns
    cols = wg.shape[1]
    scale = HD ** (-0.5)
    per = EFF // cols
    shift = per.bit_length() - 1

    qparts = 4
    qrows = D // qparts
    loads = [
        pltpu.make_async_copy(
            wqkv_hbm.at[pl.ds(i * qrows, qrows)], wqkv.at[pl.ds(i * qrows, qrows)], wsem.at[i]
        )
        for i in range(qparts)
    ]
    rest = [
        pltpu.make_async_copy(src, dst, wsem.at[qparts + i])
        for i, (src, dst) in enumerate(
            [(kc_hbm, kc), (vc_hbm, vc), (wout_hbm, wout), (wg_hbm, wg), (wu_hbm, wu), (wd_hbm, wd)]
        )
    ]
    for c in loads + rest:
        c.start()
    load_k, load_v, load_out, load_g, load_u, load_d = rest

    barrier = pltpu.get_barrier_semaphore()

    def greet(i, carry):
        d = lax.rem(me + i, devs)
        pl.semaphore_signal(
            barrier, inc=1, device_id=(d // ns, lax.rem(d, ns)), device_id_type=MESH
        )
        return carry

    lax.fori_loop(1, devs, greet, 0)

    xf = x_ref[...].astype(F32)
    a = normed(xf, again_ref[...].astype(F32)).astype(BF16)
    proj = jnp.zeros((STEPS, wqkv.shape[1]), F32)
    for i in range(qparts):
        loads[i].wait()
        proj = proj + jnp.dot(
            a[:, i * qrows : (i + 1) * qrows],
            wqkv[i * qrows : (i + 1) * qrows, :],
            preferred_element_type=F32,
        )
    cosine = rope_ref[0:STEPS, :]
    sine = rope_ref[STEPS : 2 * STEPS, :]

    def rotated(head):
        v = proj[:, head * HD : (head + 1) * HD]
        return v * cosine + pltpu.roll(v, HD // 2, 1) * sine

    for head in range(QH):
        qf[head * STEPS : (head + 1) * STEPS, :] = rotated(head)
    kf[...] = jnp.zeros_like(kf)
    vf[...] = jnp.zeros_like(vf)
    for head in range(KVH):
        kf[head * STEPS : (head + 1) * STEPS, :] = rotated(QH + head)
        vf[head * STEPS : (head + 1) * STEPS, :] = proj[
            :, (QH + KVH + head) * HD : (QH + KVH + head + 1) * HD
        ]
    own_q = qf[...].astype(BF16)
    q_all[seq] = own_q

    pl.semaphore_wait(barrier, devs - 1)

    def q_copy(peer, slot, k):
        return pltpu.make_async_remote_copy(
            src_ref=q_all.at[seq], dst_ref=q_all.at[slot], send_sem=q_s.at[k],
            recv_sem=q_r.at[slot], device_id=(req, peer), device_id_type=MESH,
        )

    def q_send(i, carry):
        peer = lax.rem(seq + i, ns)
        q_copy(peer, seq, peer).start()
        return carry

    lax.fori_loop(1, ns, q_send, 0)

    row = iota((ROWS, HD), 0)
    lane = iota((ROWS, HD), 1)
    eye = row == lane

    def to_row(col):
        return jnp.sum(jnp.where(eye, col, 0.0), axis=0, keepdims=True)

    def to_col(r):
        return jnp.sum(jnp.where(eye, r, 0.0), axis=1, keepdims=True)

    tail = (
        lax.dot_general(
            own_q, kf[...].astype(BF16), (((1,), (1,)), ((), ())), preferred_element_type=F32
        )
        * scale
    )
    upper = (row >= HALF).astype(jnp.int32)
    fresh = ((lane >> 2) == upper) & ((lane & 3) <= (row & 3))
    tail = jnp.where(fresh, tail, jnp.where(lane == KVH * STEPS, sink_ref[...], -1e30))
    tail_peak = jnp.max(tail, axis=1, keepdims=True)
    tail_w = jnp.exp(tail - tail_peak)
    tail_total = jnp.sum(tail_w, axis=1, keepdims=True)
    tail_mixed = jnp.dot(
        tail_w.astype(BF16), vf[...].astype(BF16), preferred_element_type=F32
    )

    load_k.wait()
    load_v.wait()

    first = jnp.where(row < HALF, 1.0, 0.0).astype(BF16)
    second = jnp.where(row < HALF, 0.0, 1.0).astype(BF16)
    slot_id = seq * lpos + iota((ROWS, lpos), 1)
    step_id = iota((ROWS, lpos), 0) & 3
    stat_row = iota((16, HD), 0)

    def q_wait(i, carry):
        peer = lax.rem(seq + i, ns)
        q_copy(peer, peer, peer).wait_recv()
        return carry

    lax.fori_loop(1, ns, q_wait, 0)

    def p_copy(peer, slot, k):
        return pltpu.make_async_remote_copy(
            src_ref=part.at[peer], dst_ref=part_in.at[slot], send_sem=p_s.at[k],
            recv_sem=p_r.at[slot], device_id=(req, peer), device_id_type=MESH,
        )

    def attend(n):
        q = q_all[n]
        wide = jnp.concatenate([q * first, q * second], axis=1)
        s = (
            lax.dot_general(wide, kc[n], (((1,), (1,)), ((), ())), preferred_element_type=F32)
            * scale
        )
        length = lens[n]
        back = (length - 1 - slot_id) & (window - 1)
        valid = back < jnp.minimum(length, window - 1 - step_id)
        peak = jnp.max(jnp.where(valid, s, -1e30), axis=1, keepdims=True)
        w = jnp.where(valid, jnp.exp(s - peak), 0.0)
        total = jnp.sum(w, axis=1, keepdims=True)
        both = jnp.dot(w.astype(BF16), vc[n], preferred_element_type=F32)
        mixed = jnp.where(row < HALF, both[:, :HD], both[:, HD:])
        stats = jnp.zeros((16, HD), F32)
        for k, v in enumerate(split3(to_row(peak)) + split3(to_row(total))):
            stats = jnp.where(stat_row == k, v, stats)
        return mixed.astype(BF16), stats.astype(BF16)

    group = 4

    def attend_some(b, carry):
        for j in range(group):
            n = lax.rem(seq + 1 + b * group + j, ns)
            mixed, stats = attend(n)
            part[n, 0:ROWS, :] = mixed
            part[n, ROWS:MSG, :] = stats
        for j in range(group):
            i = b * group + j
            n = lax.rem(seq + 1 + i, ns)

            @pl.when(i < ns - 1)
            def _():
                p_copy(n, seq, n).start()

        return carry

    lax.fori_loop(0, ns // group, attend_some, 0)
    part_in[seq] = part[seq]

    def p_wait(i, carry):
        peer = lax.rem(seq + i, ns)
        p_copy(peer, peer, peer).wait_recv()
        return carry

    lax.fori_loop(1, ns, p_wait, 0)

    peaks, totals = [], []
    for j in range(ns):
        st = part_in[j, ROWS:MSG, :].astype(F32)
        peaks.append(st[0:1] + st[1:2] + st[2:3])
        totals.append(st[3:4] + st[4:5] + st[5:6])
    top = to_row(tail_peak)
    for p in peaks:
        top = jnp.maximum(top, p)
    total_row = jnp.zeros((1, HD), F32)
    mixed = jnp.zeros((ROWS, HD), F32)
    for j in range(ns):
        share = jnp.exp(peaks[j] - top)
        total_row = total_row + share * totals[j]
        mixed = mixed + to_col(share) * part_in[j, 0:ROWS, :].astype(F32)
    tail_share = jnp.exp(tail_peak - to_col(top))
    denom = to_col(total_row) + tail_total * tail_share
    qf[...] = (mixed + tail_mixed * tail_share) / denom
    attn = jnp.concatenate(
        [qf[head * STEPS : (head + 1) * STEPS, :] for head in range(QH)], axis=1
    ).astype(BF16)
    load_out.wait()
    h = (xf + jnp.dot(attn, wout[...], preferred_element_type=F32)).astype(BF16).astype(F32)
    u = normed(h, mgain_ref[...].astype(F32)).astype(BF16)
    u32 = u.astype(F32)
    for g in range(UG):
        uf[g * STEPS : (g + 1) * STEPS, :] = u32[:, g * UL : (g + 1) * UL]
    rows_all[me] = uf[...].astype(BF16)

    def u_copy(slot, k, peer):
        return pltpu.make_async_remote_copy(
            src_ref=rows_all.at[slot], dst_ref=rows_all.at[slot], send_sem=u_s.at[k],
            recv_sem=u_r.at[slot], device_id=(req, peer), device_id_type=MESH,
        )

    def f_copy(slot, k):
        return pltpu.make_async_remote_copy(
            src_ref=rows_all.at[slot], dst_ref=rows_all.at[slot], send_sem=f_s.at[k],
            recv_sem=u_r.at[slot], device_id=(1 - req, seq), device_id_type=MESH,
        )

    def u_send(i, carry):
        peer = lax.rem(seq + i, ns)
        u_copy(me, peer, peer).start()
        return carry

    lax.fori_loop(1, ns, u_send, 0)
    f_copy(me, seq).start()

    rown = rown_ref[...]
    logits = jnp.dot(u, router_ref[...], preferred_element_type=F32)
    expert = iota((STEPS, E), 1)
    chosen = [
        jnp.sum(jnp.where(rown[:, k : k + 1] == expert, logits, 0.0), axis=1, keepdims=True)
        for k in range(TOP)
    ]
    peak = functools.reduce(jnp.maximum, chosen)
    raised = [jnp.exp(c - peak) for c in chosen]
    norm = functools.reduce(jnp.add, raised)
    shares = [r / norm for r in raised]

    width = blk * 16
    nblk = devs // blk
    lane4 = iota((STEPS, width), 1)
    step4 = iota((STEPS, width), 0)
    coefs = []
    for b in range(nblk):
        source = ((lane4 >> 4) + b * blk) >> shift
        hit = jnp.zeros((STEPS, width), F32)
        dense = jnp.zeros((STEPS, width), F32)
        for k in range(TOP):
            same = rown[:, k : k + 1] == source
            hit = jnp.where(same, 1.0, hit)
            dense = jnp.where(same, shares[k], dense)
        slot = jnp.zeros((STEPS, width), F32)
        for t in range(STEPS - 1):
            slot = slot + jnp.where(step4 > t, hit[t : t + 1], 0.0)
        mine = (hit > 0.0) & (slot == (lane4 & 1).astype(F32))
        dense = jnp.where(mine, dense, 0.0)
        for k, v in enumerate(split3(dense)):
            for g in range(OG):
                at = (k * OG + g) * STEPS
                coef[b, at : at + STEPS, :] = jnp.where(((lane4 & 15) >> 1) == g, v, 0.0)

    expert_mine = (me * cols) // EFF
    pick_rows = UG * blk * MOST
    prow = iota((pick_rows, width), 0)
    plane = iota((pick_rows, width), 1)
    piece = prow // (blk * MOST)
    source_row = prow & (blk * MOST - 1)
    place_ok = ((plane >> 4) == (source_row >> 1)) & (((plane & 15) >> 2) == piece)
    want = (source_row & 1).astype(F32)
    lane8 = iota((8, width), 1)
    picks = []
    for b in range(nblk):
        hit = jnp.zeros((8, width), F32)
        for k in range(TOP):
            named = jnp.broadcast_to(rall_ref[k : k + 1, b * width : (b + 1) * width], (8, width))
            hit = jnp.where(named == expert_mine, 1.0, hit)
        slot = jnp.zeros((8, width), F32)
        for t in range(1, STEPS):
            slot = slot + jnp.where((lane8 & 3) >= t, pltpu.roll(hit, t, 1), 0.0)
        code = jnp.where(hit > 0.0, slot, -1.0)[0:1]
        picks.append(jnp.where(place_ok & (code == want), 1.0, 0.0).astype(BF16))

    out_rows = iota((width, OG * blk * MOST), 0)
    out_lane = iota((width, OG * blk * MOST), 1)
    out_piece = out_lane // (blk * MOST)
    out_source = out_lane & (blk * MOST - 1)
    spread = jnp.where(
        ((out_rows >> 4) == (out_source >> 1))
        & ((out_rows & 15) == out_piece * MOST + (out_source & 1)),
        1.0,
        0.0,
    ).astype(BF16)

    def u_wait(i, carry):
        peer = lax.rem(seq + i, ns)
        u_copy(req * ns + peer, peer, peer).wait_recv()
        f_copy(req * ns + peer, peer).start()
        return carry

    lax.fori_loop(1, ns, u_wait, 0)

    def f_wait(i, carry):
        peer = lax.rem(seq + i, ns)
        f_copy((1 - req) * ns + peer, peer).wait_recv()
        return carry

    lax.fori_loop(0, ns, f_wait, 0)

    taken = []
    for b in range(nblk):
        got = jnp.dot(
            picks[b],
            rows_all[b * blk : (b + 1) * blk].reshape(width, UL),
            preferred_element_type=F32,
        ).astype(BF16)
        taken.append(
            jnp.concatenate(
                [got[g * blk * MOST : (g + 1) * blk * MOST] for g in range(UG)], axis=1
            )
        )
    taken = jnp.concatenate(taken, axis=0) if nblk > 1 else taken[0]
    load_g.wait()
    load_u.wait()
    load_d.wait()
    gate = jnp.dot(taken, wg[...], preferred_element_type=F32)
    hidden = jnp.maximum(gate, 0.0) * jnp.dot(taken, wu[...], preferred_element_type=F32)
    made = jnp.dot(hidden.astype(BF16), wd[...], preferred_element_type=F32).astype(BF16)
    for b in range(nblk):
        stacked = jnp.concatenate(
            [
                made[b * blk * MOST : (b + 1) * blk * MOST, g * OL : (g + 1) * OL]
                for g in range(OG)
            ],
            axis=0,
        )
        prod_out[b * blk : (b + 1) * blk] = (
            jnp.dot(spread, stacked, preferred_element_type=F32).astype(BF16).reshape(blk, 16, OL)
        )

    def o_copy(d, slot, k):
        return pltpu.make_async_remote_copy(
            src_ref=prod_out.at[d], dst_ref=prod_in.at[slot], send_sem=o_s.at[k],
            recv_sem=o_r.at[slot], device_id=(d // ns, lax.rem(d, ns)), device_id_type=MESH,
        )

    def o_send(i, carry):
        d = lax.rem(me + i, devs)
        o_copy(d, me, d).start()
        return carry

    lax.fori_loop(1, devs, o_send, 0)
    prod_in[me] = prod_out[me]

    def o_wait(i, carry):
        d = lax.rem(me + i, devs)
        o_copy(d, d, d).wait_recv()
        return carry

    lax.fori_loop(1, devs, o_wait, 0)

    moe = jnp.zeros((3 * OG * STEPS, OL), F32)
    for b in range(nblk):
        moe = moe + jnp.dot(
            coef[b].astype(BF16),
            prod_in[b * blk : (b + 1) * blk].reshape(width, OL),
            preferred_element_type=F32,
        )
    span = OG * STEPS
    moe = moe[0:span] + moe[span : 2 * span] + moe[2 * span : 3 * span]
    moe = jnp.concatenate([moe[g * STEPS : (g + 1) * STEPS] for g in range(OG)], axis=1)
    out_ref[...] = (h + moe).astype(BF16)

    def drain(i, carry):
        peer = lax.rem(seq + i, ns)
        q_copy(peer, seq, peer).wait_send()
        p_copy(peer, seq, peer).wait_send()
        u_copy(me, peer, peer).wait_send()
        f_copy(req * ns + peer, peer).wait_send()
        return carry

    lax.fori_loop(1, ns, drain, 0)
    f_copy(me, seq).wait_send()

    def o_drain(i, carry):
        d = lax.rem(me + i, devs)
        o_copy(d, me, d).wait_send()
        return carry

    lax.fori_loop(1, devs, o_drain, 0)


def on_device(
    nr, ns, tokens, lengths, k_cache, v_cache, attn_gain, w_qkv, sink, w_out, moe_gain, router,
    w_gate, w_up, w_down, routes,
):
    seq = lax.axis_index("seq")
    device = lax.axis_index("req") * ns + seq
    devs = nr * ns
    blk = min(BLK, devs)
    lpos = k_cache.shape[1]
    group = lengths.shape[0]
    cols = w_gate.shape[1]
    half = HD // 2
    own_len = lax.dynamic_slice_in_dim(lengths, seq, 1)
    place = own_len + jnp.arange(STEPS, dtype=jnp.int32)
    inverse = jnp.exp(-jnp.log(1000000.0) * 2.0 * jnp.arange(half, dtype=F32) / HD)
    angle = place.astype(F32)[:, None] * inverse
    cosine, sine = jnp.cos(angle), jnp.sin(angle)
    rope = jnp.concatenate(
        [jnp.concatenate([cosine, cosine], 1), jnp.concatenate([-sine, sine], 1)], 0
    )
    sinks = jnp.broadcast_to(jnp.repeat(sink, STEPS)[:, None], (ROWS, HD))
    rall = jnp.broadcast_to(
        routes.transpose(2, 0, 1)[:, :, None, :], (TOP, devs, 4, STEPS)
    ).reshape(TOP, devs * 16)
    rown = lax.dynamic_index_in_dim(routes, device, 0, False)

    vmem = pl.BlockSpec(memory_space=pltpu.VMEM)
    smem = pl.BlockSpec(memory_space=pltpu.SMEM)
    hbm = pl.BlockSpec(memory_space=pl.ANY)
    dma = pltpu.SemaphoreType.DMA
    out = pl.pallas_call(
        functools.partial(kernel, nr, ns, blk),
        out_shape=jax.ShapeDtypeStruct((STEPS, D), BF16),
        in_specs=[smem] + [vmem] * 8 + [hbm] * 7,
        out_specs=vmem,
        scratch_shapes=[
            pltpu.VMEM(w_qkv.shape, BF16),
            pltpu.VMEM(w_out.shape, BF16),
            pltpu.VMEM(w_gate.shape, BF16),
            pltpu.VMEM(w_up.shape, BF16),
            pltpu.VMEM(w_down.shape, BF16),
            pltpu.VMEM((group, lpos, KVH * HD), BF16),
            pltpu.VMEM((group, lpos, KVH * HD), BF16),
            pltpu.VMEM((ROWS, HD), F32),
            pltpu.VMEM((HD, HD), F32),
            pltpu.VMEM((HD, HD), F32),
            pltpu.VMEM((ns, ROWS, HD), BF16),
            pltpu.VMEM((ns, MSG, HD), BF16),
            pltpu.VMEM((ns, MSG, HD), BF16),
            pltpu.VMEM((UG * STEPS, UL), F32),
            pltpu.VMEM((devs, UG * STEPS, UL), BF16),
            pltpu.VMEM((devs, 16, OL), BF16),
            pltpu.VMEM((devs, 16, OL), BF16),
            pltpu.VMEM((devs // blk, 3 * OG * STEPS, blk * 16), F32),
            dma((10,)), dma((ns,)), dma((ns,)), dma((ns,)), dma((ns,)), dma((ns,)),
            dma((devs,)), dma((ns,)), dma((devs,)), dma((devs,)),
        ],
        compiler_params=pltpu.CompilerParams(
            collective_id=0, has_side_effects=True, vmem_limit_bytes=56 * 1024 * 1024
        ),
    )(
        lengths, tokens.reshape(STEPS, D), attn_gain.reshape(1, D), moe_gain.reshape(1, D), rope,
        sinks, rall, rown, router, k_cache, v_cache, w_qkv, w_out, w_gate, w_up, w_down,
    )
    return out.reshape(STEPS, 1, D)


def solution(mesh):
    nr, ns = mesh.shape["req"], mesh.shape["seq"]
    in_specs = (
        P(None, ("req", "seq"), None),
        P("req"),
        P("req", "seq", None),
        P("req", "seq", None),
        P(),
        P(),
        P(),
        P(),
        P(),
        P(),
        P(None, ("req", "seq")),
        P(None, ("req", "seq")),
        P(("req", "seq"), None),
        P(),
    )
    out_specs = P(None, ("req", "seq"), None)
    return jax.shard_map(
        functools.partial(on_device, nr, ns),
        mesh=mesh,
        in_specs=in_specs,
        out_specs=out_specs,
        check_vma=False,
    )
```

time: 413 us -> 56.4 us (0.14)
  blocking collectives: 189 us -> 0 us
  waiting for transfers between devices: 127 us -> 0 us
  Pallas kernels: 0 us -> 42.8 us
  other arithmetic: 34.5 us -> 1.44 us
  matrix products: 20.3 us -> 0 us
  local copies, waits for them, and re-layouts: 26.8 us -> 11.6 us
  between operations: 13.8 us -> 0.03 us
    all_gather x4 -> x0, blocking collectives: 189 us -> none  [the longest x2 77.3 us: combined_all(): lax.all_gather(a.astype(kind), axis)]
    unnamed x3 -> x0, waiting for transfers between devices: 127 us -> none
    pallas_call x0 -> x1, Pallas kernels: none -> 42.8 us  [on_device(): pl.pallas_call(functools.partial(kernel, nr, ns, blk), out_shape=jax.Shap...]
    add x31 -> x0, other arithmetic: 22.8 us -> none  [the longest x15 21.7 us: combine_parts(): first[2] * left_scale[..., None] + second[2] * right_scale[..., None]]
    dot_general x12 -> x0, matrix products: 20.3 us -> none  [the longest x1 3.77 us: on_device(): jnp.einsum('srm,mn->srn', a, w_qkv, preferred_element_type=jnp.float32)]
    reshape x5 -> x3, local copies, waits for them, and re-layouts: 9.46 us -> 3.43 us  [the longest x1 1.29 us: on_device(): attn_gain.reshape(1, D)]
    convert_element_type x10 -> x1, other arithmetic: 5.88 us -> 0.65 us  [on_device(): angle = place.astype(F32)[:, None] * inverse]
  transfers between devices with their start and end apart: 2 -> 0, of which waited for: 1 -> 0; matrix products, arithmetic and copies ran while one was open for 4% -> 0% of each run, Pallas kernels for 0% -> 0%
where the time goes in v1:
time: 56.4 us; the launch traced here: 55.9 us
  Pallas kernels  42.8 us (76%)
  local copies, waits for them, and re-layouts  11.6 us (21%)
  other arithmetic  1.44 us (3%)
    pallas_call x1, Pallas kernels, on_device(): pl.pallas_call(functools.partial(kernel, nr, ns, blk), out_shape=jax.Shap...  42.8 us
    unnamed x2, local copies, waits for them, and re-layouts  3.12 us
    dynamic_slice x1, local copies, waits for them, and re-layouts, on_device(): rown = lax.dynamic_index_in_dim(routes, device, 0, False)  1.5 us
    broadcast_in_dim x3, local copies, waits for them, and re-layouts, on_device(): sinks = jnp.broadcast_to(jnp.repeat(sink, STEPS)[:, None], (ROWS, HD))  1.49 us
    reshape x1, local copies, waits for them, and re-layouts, on_device(): attn_gain.reshape(1, D)  1.29 us
    reshape x1, local copies, waits for them, and re-layouts, on_device(): moe_gain.reshape(1, D)  1.28 us
    dynamic_slice x1, local copies, waits for them, and re-layouts, on_device(): own_len = lax.dynamic_slice_in_dim(lengths, seq, 1)  1.24 us

profile of v1, /device:TPU:0, one launch (start us, length us, event | category | flops | bytes accessed | tf_op | source)
XLA Modules:
  0.0 55.9 jit_solution(15918353689206891789)
XLA Ops:
  0.0 1.2 %dynamic_slice.7 = s32[1]{0:T(128)} dynamic-slice(s32[16]{0:T(128)} %lens.1, s32[]{:T(128)S(6)} %select_n.7), dynamic_slice_sizes={1} | dynamic-slice | bytes 12 | tf_op jit(solution)/shard_map/dynamic_slice | solution.py:461
  1.2 0.6 %add_convert_fusion = f32[4]{0:T(128)S(1)} fusion(s32[]{:T(128)} %bitcast.1), kind=kLoop, calls=%fused_computation.5 | loop fusion | flops 8 | bytes 20 | tf_op jit(solution)/shard_map/convert_element_type | solution.py:464
  1.9 1.5 %dynamic-slice_reduce_fusion.rown_ref = s32[4,4]{1,0:T(4,128)} fusion(s32[32,4,4]{0,2,1:T(4,128)} %param.27, s32[]{:T(128)S(6)} %select_n.8), kind=kLoop, calls=%fused_computation | loop fusion | bytes 132 | tf_op jit(solution)/shard_map/jit(dynamic_index_in_dim)/dynamic_slice | solution.py:473
  3.4 0.1 multiply_cosine_fusion
  3.5 0.7 %maximum_maximum_fusion.rope_ref = f32[8,128]{1,0:T(8,128)} fusion(f32[4,64]{1,0:T(4,128)S(1)} %get-tuple-element.7, f32[4,64]{1,0:T(4,128)S(1)} %get-tuple-element.6, f32[4,64]{1,0:T(4,128)S(1)} %get-tuple-element.5), kind=kLoop, calls=%fused_computation.1 | loop fusion | flops 3072 | bytes 7168 | tf_op jit(solution)/shard_map/concatenate | solution.py:466
  4.2 1.3 %reshape.28.again_ref = bf16[1,1536]{1,0:T(2,128)(2,1)} reshape(bf16[1536]{0:T(1024)(128)(2,1)} %param.18) | data formatting | bytes 6144 | tf_op jit(solution)/shard_map/reshape | solution.py:510
  5.5 1.3 %reshape.29.mgain_ref = bf16[1,1536]{1,0:T(2,128)(2,1)} reshape(bf16[1536]{0:T(1024)(128)(2,1)} %param.22) | data formatting | bytes 6144 | tf_op jit(solution)/shard_map/reshape | solution.py:510
  6.8 0.7 %broadcast_in_dim.8 = f32[12,4]{1,0:T(8,128)S(1)} broadcast(f32[12]{0:T(128)} %param.20), dimensions={0} | broadcast | bytes 240 | tf_op jit(solution)/shard_map/broadcast_in_dim | solution.py:469
  7.5 0.1 broadcast_in_dim.9
  7.6 0.7 %broadcast_in_dim.20.sink_ref = f32[48,128]{1,0:T(8,128)} broadcast(f32[48]{0:T(128)S(1)} %broadcast_in_dim.9), dimensions={0} | broadcast | bytes 24768 | tf_op jit(solution)/shard_map/broadcast_in_dim | solution.py:469
  8.2 0.8 %copy.17 = s32[4,32,4]{2,1,0:T(8,128)S(1)} copy(s32[4,32,4]{1,0,2:T(4,128)} %bitcast.5) | data formatting | bytes 4096 | tf_op jit(solution)/shard_map/transpose | solution.py:471
  9.1 0.9 %reshape.30.rall_ref = s32[4,512]{1,0:T(4,128)} reshape(s32[4,32,4,4]{3,2,1,0:T(4,128)S(1)} %broadcast_in_dim.21) | data formatting | bytes 16384 | tf_op jit(solution)/shard_map/reshape | solution.py:472
  10.0 1.8 %copy.18.router_ref = bf16[1536,32]{1,0:T(8,128)(2,1)} copy(bf16[1536,32]{0,1:T(8,128)(2,1)} %param.23) | data formatting | bytes 196608 | tf_op args[9]
  11.8 42.8 %shard_map.136 = bf16[4,1536]{1,0:T(4,128)(2,1)} custom-call(s32[16]{0:T(128)} %lens.1, bf16[4,1536]{1,0:T(4,128)(2,1)} %bitcast.6, bf16[1,1536]{1,0:T(2,128)(2,1)} %reshape.28.again_ref, bf16[1,1536]{1,0:T(2,128)(2,1)} %reshape.29.mgain_ref, f32[8,128]{1,0:T(8,128)} %maximum_maximum_fusion.rope_ref, f32[48,128]{1,0:T(8,128)} %broadcast_in_dim.20.sink_ref, ...), custom_call_target="tpu_custom_call" | custom-call | tf_op jit(solution)/shard_map/pallas_call | solution.py:479
  54.6 1.3 %copy.20 = bf16[4,1,1536]{2,0,1:T(4,128)(2,1)} copy(bf16[4,1,1536]{2,0,1:T(4,128)(2,1)} %bitcast.4) | data formatting | bytes 24576
  (2 shorter events, 0.1 us)

commit v2 on v1

--- a/solution.py
+++ b/solution.py
@@ -46,7 +46,7 @@
 
 
 def kernel(
-    nr, ns, blk, lens, x_ref, again_ref, mgain_ref, rope_ref, sink_ref, rall_ref, rown_ref, router_ref,
+    nr, ns, blk, lens, sinks, x_ref, again_ref, mgain_ref, rope_ref, rall_ref, router_ref,
     kc_hbm, vc_hbm, wqkv_hbm, wout_hbm, wg_hbm, wu_hbm, wd_hbm,
     out_ref,
     wqkv, wout, wg, wu, wd, kc, vc,
@@ -94,7 +94,7 @@
     lax.fori_loop(1, devs, greet, 0)
 
     xf = x_ref[...].astype(F32)
-    a = normed(xf, again_ref[...].astype(F32)).astype(BF16)
+    a = normed(xf, again_ref[...].astype(F32).reshape(1, D)).astype(BF16)
     proj = jnp.zeros((STEPS, wqkv.shape[1]), F32)
     for i in range(qparts):
         loads[i].wait()
@@ -103,8 +103,9 @@
             wqkv[i * qrows : (i + 1) * qrows, :],
             preferred_element_type=F32,
         )
-    cosine = rope_ref[0:STEPS, :]
-    sine = rope_ref[STEPS : 2 * STEPS, :]
+    rope = rope_ref[seq]
+    cosine = rope[0:STEPS]
+    sine = rope[STEPS : 2 * STEPS]
 
     def rotated(head):
         v = proj[:, head * HD : (head + 1) * HD]
@@ -154,8 +155,11 @@
         * scale
     )
     upper = (row >= HALF).astype(jnp.int32)
+    sink_rows = jnp.zeros((ROWS, HD), F32)
+    for head in range(QH):
+        sink_rows = jnp.where((row >> 2) == head, sinks[head], sink_rows)
     fresh = ((lane >> 2) == upper) & ((lane & 3) <= (row & 3))
-    tail = jnp.where(fresh, tail, jnp.where(lane == KVH * STEPS, sink_ref[...], -1e30))
+    tail = jnp.where(fresh, tail, jnp.where(lane == KVH * STEPS, sink_rows, -1e30))
     tail_peak = jnp.max(tail, axis=1, keepdims=True)
     tail_w = jnp.exp(tail - tail_peak)
     tail_total = jnp.sum(tail_w, axis=1, keepdims=True)
@@ -255,7 +259,7 @@
     ).astype(BF16)
     load_out.wait()
     h = (xf + jnp.dot(attn, wout[...], preferred_element_type=F32)).astype(BF16).astype(F32)
-    u = normed(h, mgain_ref[...].astype(F32)).astype(BF16)
+    u = normed(h, mgain_ref[...].astype(F32).reshape(1, D)).astype(BF16)
     u32 = u.astype(F32)
     for g in range(UG):
         uf[g * STEPS : (g + 1) * STEPS, :] = u32[:, g * UL : (g + 1) * UL]
@@ -281,11 +285,20 @@
     lax.fori_loop(1, ns, u_send, 0)
     f_copy(me, seq).start()
 
-    rown = rown_ref[...]
-    logits = jnp.dot(u, router_ref[...], preferred_element_type=F32)
-    expert = iota((STEPS, E), 1)
+    every = (STEPS, devs * 16)
+    own_lane = iota(every, 1) == me * 16 + iota(every, 0)
+    rown = [
+        jnp.sum(
+            jnp.where(own_lane, rall_ref[k : k + 1, :].astype(F32), 0.0), axis=1, keepdims=True
+        )
+        for k in range(TOP)
+    ]
+    logits = lax.dot_general(
+        u, router_ref[...], (((1,), (1,)), ((), ())), preferred_element_type=F32
+    )
+    expert = iota((STEPS, E), 1).astype(F32)
     chosen = [
-        jnp.sum(jnp.where(rown[:, k : k + 1] == expert, logits, 0.0), axis=1, keepdims=True)
+        jnp.sum(jnp.where(rown[k] == expert, logits, 0.0), axis=1, keepdims=True)
         for k in range(TOP)
     ]
     peak = functools.reduce(jnp.maximum, chosen)
@@ -299,11 +312,11 @@
     step4 = iota((STEPS, width), 0)
     coefs = []
     for b in range(nblk):
-        source = ((lane4 >> 4) + b * blk) >> shift
+        source = (((lane4 >> 4) + b * blk) >> shift).astype(F32)
         hit = jnp.zeros((STEPS, width), F32)
         dense = jnp.zeros((STEPS, width), F32)
         for k in range(TOP):
-            same = rown[:, k : k + 1] == source
+            same = rown[k] == source
             hit = jnp.where(same, 1.0, hit)
             dense = jnp.where(same, shares[k], dense)
         slot = jnp.zeros((STEPS, width), F32)
@@ -450,27 +463,21 @@
     nr, ns, tokens, lengths, k_cache, v_cache, attn_gain, w_qkv, sink, w_out, moe_gain, router,
     w_gate, w_up, w_down, routes,
 ):
-    seq = lax.axis_index("seq")
-    device = lax.axis_index("req") * ns + seq
     devs = nr * ns
     blk = min(BLK, devs)
     lpos = k_cache.shape[1]
     group = lengths.shape[0]
-    cols = w_gate.shape[1]
     half = HD // 2
-    own_len = lax.dynamic_slice_in_dim(lengths, seq, 1)
-    place = own_len + jnp.arange(STEPS, dtype=jnp.int32)
-    inverse = jnp.exp(-jnp.log(1000000.0) * 2.0 * jnp.arange(half, dtype=F32) / HD)
-    angle = place.astype(F32)[:, None] * inverse
-    cosine, sine = jnp.cos(angle), jnp.sin(angle)
-    rope = jnp.concatenate(
-        [jnp.concatenate([cosine, cosine], 1), jnp.concatenate([-sine, sine], 1)], 0
-    )
-    sinks = jnp.broadcast_to(jnp.repeat(sink, STEPS)[:, None], (ROWS, HD))
+    shape = (group, 2 * STEPS, HD)
+    row, lane = iota(shape, 1), iota(shape, 2)
+    index = (lane & (half - 1)).astype(F32)
+    inverse = jnp.exp(-jnp.log(1000000.0) * 2.0 * index / HD)
+    angle = (lengths[:, None, None] + (row & (STEPS - 1))).astype(F32) * inverse
+    sine = jnp.sin(angle)
+    rope = jnp.where(row < STEPS, jnp.cos(angle), jnp.where(lane < half, -sine, sine))
     rall = jnp.broadcast_to(
         routes.transpose(2, 0, 1)[:, :, None, :], (TOP, devs, 4, STEPS)
     ).reshape(TOP, devs * 16)
-    rown = lax.dynamic_index_in_dim(routes, device, 0, False)
 
     vmem = pl.BlockSpec(memory_space=pltpu.VMEM)
     smem = pl.BlockSpec(memory_space=pltpu.SMEM)
@@ -479,7 +486,7 @@
     out = pl.pallas_call(
         functools.partial(kernel, nr, ns, blk),
         out_shape=jax.ShapeDtypeStruct((STEPS, D), BF16),
-        in_specs=[smem] + [vmem] * 8 + [hbm] * 7,
+        in_specs=[smem] * 2 + [vmem] * 6 + [hbm] * 7,
         out_specs=vmem,
         scratch_shapes=[
             pltpu.VMEM(w_qkv.shape, BF16),
@@ -507,8 +514,7 @@
             collective_id=0, has_side_effects=True, vmem_limit_bytes=56 * 1024 * 1024
         ),
     )(
-        lengths, tokens.reshape(STEPS, D), attn_gain.reshape(1, D), moe_gain.reshape(1, D), rope,
-        sinks, rall, rown, router, k_cache, v_cache, w_qkv, w_out, w_gate, w_up, w_down,
+        lengths, sink, tokens.reshape(STEPS, D), attn_gain, moe_gain, rope, rall, router.T, k_cache, v_cache, w_qkv, w_out, w_gate, w_up, w_down,
     )
     return out.reshape(STEPS, 1, D)
 

time: 56.4 us -> 47.7 us (0.85)
  local copies, waits for them, and re-layouts: 11.6 us -> 3.02 us
    dynamic_slice x2 -> x0, local copies, waits for them, and re-layouts: 2.74 us -> none  [the longest x1 1.5 us: on_device(): rown = lax.dynamic_index_in_dim(routes, device, 0, False)]
    reshape x2 -> x0, local copies, waits for them, and re-layouts: 2.57 us -> none  [the longest x1 1.29 us: on_device(): attn_gain.reshape(1, D)]
    unnamed x2 -> x1, local copies, waits for them, and re-layouts: 3.12 us -> 1.31 us
    select_n x0 -> x1, other arithmetic: none -> 1.6 us  [on_device(): jnp.where(row < STEPS, jnp.cos(angle), jnp.where(lane < half, -sine, sine))]
    broadcast_in_dim x3 -> x0, local copies, waits for them, and re-layouts: 1.49 us -> none  [on_device(): sinks = jnp.broadcast_to(jnp.repeat(sink, STEPS)[:, None], (ROWS, HD))]
    concatenate x1 -> x0, other arithmetic: 0.67 us -> none  [on_device(): jnp.concatenate([jnp.concatenate([cosine, cosine], 1), jnp.concatenate([-...]
    convert_element_type x1 -> x0, other arithmetic: 0.65 us -> none  [on_device(): angle = place.astype(F32)[:, None] * inverse]
where the time goes in v2:
time: 47.7 us; the launch traced here: 47.4 us
  Pallas kernels  42.7 us (90%)
  local copies, waits for them, and re-layouts  3.02 us (6%)
  other arithmetic  1.62 us (3%)
    pallas_call x1, Pallas kernels, on_device(): pl.pallas_call(functools.partial(kernel, nr, ns, blk), out_shape=jax.Shap...  42.7 us
    select_n x1, other arithmetic, on_device(): jnp.where(row < STEPS, jnp.cos(angle), jnp.where(lane < half, -sine, sine))  1.6 us
    unnamed x1, local copies, waits for them, and re-layouts  1.31 us

profile of v2, /device:TPU:0, one launch (start us, length us, event | category | flops | bytes accessed | tf_op | source)
XLA Modules:
  0.0 47.4 jit_solution(14749659079076296661)
XLA Ops:
  0.0 0.8 %copy.16 = s32[4,32,4]{2,1,0:T(8,128)S(1)} copy(s32[4,32,4]{1,0,2:T(4,128)} %bitcast.7) | data formatting | bytes 4096 | tf_op jit(solution)/shard_map/transpose | solution.py:479
  0.8 0.9 %reshape.12.rall_ref = s32[4,512]{1,0:T(4,128)} reshape(s32[4,32,4,4]{3,2,1,0:T(4,128)S(1)} %broadcast_in_dim.2) | data formatting | bytes 16384 | tf_op jit(solution)/shard_map/reshape | solution.py:480
  1.7 1.6 %fusion.rope_ref = f32[16,8,128]{2,1,0:T(8,128)} fusion(f32[128]{0:T(128)S(1)} %multiply_exponential_fusion, s32[8]{0:T(128)S(1)} %iota_and_fusion, s32[16]{0:T(128)} %lens.1, pred[8]{0:T(512)(128)(4,1)S(1)} %iota_compare_fusion.1, pred[128]{0:T(512)(128)(4,1)S(1)} %iota_compare_fusion), kind=kLoop, calls=%fused_computation.1 | loop fusion | flops 98304 | bytes 66280 | tf_op jit(solution)/shard_map/jit(_where)/select_n | solution.py:477
  3.3 42.7 %shard_map.136 = bf16[4,1536]{1,0:T(4,128)(2,1)} custom-call(s32[16]{0:T(128)} %lens.1, f32[12]{0:T(128)} %sinks.1, bf16[4,1536]{1,0:T(4,128)(2,1)} %bitcast.6, bf16[1536]{0:T(1024)(128)(2,1)} %again_ref.1, bf16[1536]{0:T(1024)(128)(2,1)} %mgain_ref.1, f32[16,8,128]{2,1,0:T(8,128)} %fusion.rope_ref, s32[4,512]{1,0:T(4,128)} %reshape.12.rall_ref, ...), custom_call_target="tpu_custom_call" | custom-call | tf_op jit(solution)/shard_map/pallas_call | solution.py:486
  46.1 1.3 %copy.18 = bf16[4,1,1536]{2,0,1:T(4,128)(2,1)} copy(bf16[4,1,1536]{2,0,1:T(4,128)(2,1)} %bitcast.5) | data formatting | bytes 24576
  (5 shorter events, 0.1 us)
